TPU v7x, 256 devices: a whole 4x4x8 slice. The times are simulated.
256 devices in a mesh: band: 32 (over z, x), gvec: 8 (over y, core).
Axes of the slice: x: 4, y: 4, z: 8, core: 2. Of those that a mesh axis runs over, the one named last changes fastest.
Arguments:
- pairs: bfloat16 [32, 8, 512, 640], P(None, 'gvec', 'band'), may hold values from -0.59765625 to 0.59765625
- cond_energy: float32 [512], replicated, may hold values from 0.5 to 12
- val_energy: float32 [32, 8], replicated, may hold values from -12 to -2
- band_counts: int32 [32], replicated, may hold values from 1 to 16, as said below
- slab: int32 [1], replicated, may hold values from 0 to 31
Outputs:
- chi_zero: float32 [20480, 20480], P('gvec', 'band')
Inputs may be any that keep to these rules, and one draw needn't show every extreme that they name: `band_counts`: every owner has at least one occupied slot, and in every draw some owner has all 16 slots occupied.
All inputs are finite; a program needn't handle non-finite values.
Results may differ from a plain program's by a relative error of at most 0.0028.
Values may be sent and summed in bfloat16 or wider, within the bound.
No kernel may reach another device: no remote copies, remote signals or barrier semaphores. Data moves between devices by JAX's collectives and lax.ppermute only.
A program may use at most 128 MiB of HBM per device.

v0:
```python
import jax
import jax.numpy as jnp
from jax import lax
from jax.sharding import PartitionSpec as P


def on_device(pairs, cond_energy, val_energy, band_counts, slab):
    n_band = lax.axis_size("band")
    n_gvec = lax.axis_size("gvec")
    ratio = n_band // n_gvec
    local_v = pairs.shape[1]
    slot_count = pairs.shape[2]
    col_width = pairs.shape[3]
    energies = lax.dynamic_index_in_dim(val_energy, slab[0], 0, keepdims=False)
    slots = jnp.arange(slot_count, dtype=jnp.int32)
    live = (slots[None, :] < band_counts[:, None]).reshape(-1)
    weight = jnp.where(
        live[None, :], 2.0 / (energies[:, None] - cond_energy[None, :]), jnp.float32(0.0)
    )
    blocked = pairs.reshape(n_gvec, ratio, local_v, slot_count, col_width)
    by_block = lax.all_to_all(blocked, "gvec", split_axis=0, concat_axis=2, tiled=True)
    rows_all = lax.all_gather(by_block, "band", axis=3, tiled=True)[0]
    by_column = lax.all_to_all(pairs, "band", split_axis=0, concat_axis=2, tiled=True)
    cols_all = lax.all_gather(by_column, "gvec", axis=1, tiled=True)[0]
    scaled = (weight[:, :, None] * cols_all.astype(jnp.float32)).astype(jnp.bfloat16)
    result = lax.dot_general(
        rows_all, scaled, (((1, 2), (0, 1)), ((), ())), preferred_element_type=jnp.float32
    )
    return result.reshape(ratio * col_width, col_width)


def solution(mesh):
    in_specs = (P(None, "gvec", "band", None), P(), P(), P(), P())
    out_specs = P("gvec", "band")
    return jax.shard_map(
        on_device, mesh=mesh, in_specs=in_specs, out_specs=out_specs, check_vma=False
    )
```

profile of v0, /device:TPU:1, one launch (start us, length us, event | category | flops | bytes accessed | tf_op | source)
XLA Modules:
  0.0 263.4 jit_solution(6837848196494836438)
XLA Ops:
  6.5 0.0 copy-start
  6.5 0.0 all-gather.6.cloned.1.call-start
  6.5 17.7 %all_to_all.30 = bf16[8,4,1,16,640]{4,3,2,1,0:T(8,128)(2,1)S(1)} all-to-all(bf16[8,4,1,16,640]{4,3,2,1,0:T(8,128)(2,1)} %bitcast.24), channel_id=1, replica_groups=mesh['band'=32,'gvec'=8] {'gvec'}, dimensions={0} | all-to-all | bytes 1310720 | tf_op jit(solution)/shard_map/all_to_all | solution.py:21
  24.3 1.2 copy.8
  25.5 0.0 all-gather.6.cloned.1.call-update
  25.5 0.0 all-gather.4.cloned.1.call-start
  25.6 32.6 %all_to_all.31 = bf16[32,1,16,640]{3,2,1,0:T(8,128)(2,1)} all-to-all(bf16[32,1,16,640]{3,2,1,0:T(8,128)(2,1)} %param.5), channel_id=1, replica_groups=mesh['band'=32,'gvec'=8] {'band'}, dimensions={0} | all-to-all | bytes 1310720 | tf_op jit(solution)/shard_map/all_to_all | solution.py:23
  58.2 0.0 all-gather.4.cloned.1.call-update
  58.8 0.7 iota_compare_fusion
  59.6 0.1 lt.27
  59.7 0.0 copy-done
  59.7 0.2 dynamic-slice_reduce_fusion
  59.8 0.8 divide_select_fusion
  60.6 133.8 %all-gather.6.cloned.1.call-done = bf16[1,4,8,1,512,640]{5,2,3,1,0,4:T(8,128)(2,1)} async-done(((bf16[1,4,8,1,16,640]{5,2,3,1,0,4:T(8,128)(2,1)}), bf16[1,4,8,1,512,640]{5,2,3,1,0,4:T(8,128)(2,1)}) %all-gather.6.cloned.1.call-update) | async-done | bytes 20971536 | tf_op jit(solution)/shard_map/all_gather | solution.py:22
  194.4 30.2 %copy.9 = bf16[1,4,8,1,512,640]{4,5,2,1,3,0:T(8,128)(2,1)} copy(bf16[1,4,8,1,512,640]{5,2,3,1,0,4:T(8,128)(2,1)} %all-gather.6.cloned.1.call-done) | data formatting | bytes 41943040 | tf_op jit(solution)/shard_map/all_gather | solution.py:22
  224.6 8.6 %all-gather.4.cloned.1.call-done = bf16[1,8,512,640]{3,2,0,1:T(8,128)(2,1)} async-done(((bf16[1,1,512,640]{3,2,0,1:T(8,128)(2,1)}), bf16[1,8,512,640]{3,2,0,1:T(8,128)(2,1)}) %all-gather.4.cloned.1.call-update) | async-done | bytes 5242896 | tf_op jit(solution)/shard_map/all_gather | solution.py:24
  233.3 23.3 %fusion = f32[640,4,640,1]{0,2,3,1:T(8,128)} fusion(bf16[1,4,8,1,512,640]{4,5,2,1,3,0:T(8,128)(2,1)} %copy.9, bf16[1,8,512,640]{3,2,0,1:T(8,128)(2,1)} %all-gather.4.cloned.1.call-done, f32[8,512]{1,0:T(8,128)S(1)} %divide_select_fusion), kind=kOutput, calls=%fused_computation | convolution fusion | flops 13429637120 | bytes 32784384 | tf_op jit(solution)/shard_map/dot_general | solution.py:26
Async XLA Ops:
  6.5 53.1 %copy-start = (f32[32,8]{0,1:T(8,128)S(1)}, f32[32,8]{0,1:T(8,128)}, u32[]{:S(2)}) copy-start(f32[32,8]{0,1:T(8,128)} %param.7) | copy-start | bytes 3076
  6.5 187.9 %all-gather.6.cloned.1.call-start = ((), (), s32[]{:S(2)}) async-start(), calls=%async_computation.3 | async-start | bytes 21626880 | tf_op jit(solution)/shard_map/all_gather | solution.py:22
  25.5 207.7 %all-gather.4.cloned.1.call-start = ((), (), s32[]{:S(2)}) async-start(), calls=%async_computation.2 | async-start | bytes 5898240 | tf_op jit(solution)/shard_map/all_gather | solution.py:24
Sparse Core Ops, SparseCore 0:
  25.6 168.7 all-gather.5
  196.3 36.9 all-gather.3
where the time goes:
time: 264 us; the launch traced here: 263 us
  waiting for transfers between devices  142 us (54%)
  blocking collectives  50.3 us (19%)
  local copies, waits for them, and re-layouts  31.7 us (12%)
  matrix products  23.3 us (9%)
  between operations  14.1 us (5%)
    all_gather x1, waiting for transfers between devices, on_device(): rows_all = lax.all_gather(by_block, 'band', axis=3, tiled=True)[0]  134 us
    all_to_all x1, blocking collectives, on_device(): lax.all_to_all(pairs, 'band', split_axis=0, concat_axis=2, tiled=True)  32.6 us
    all_gather x1, local copies, waits for them, and re-layouts, on_device(): rows_all = lax.all_gather(by_block, 'band', axis=3, tiled=True)[0]  30.2 us
    dot_general x1, matrix products, on_device(): lax.dot_general(rows_all, scaled, (((1, 2), (0, 1)), ((), ())), preferred...  23.3 us
    all_to_all x1, blocking collectives, on_device(): lax.all_to_all(blocked, 'gvec', split_axis=0, concat_axis=2, tiled=True)  17.7 us
    all_gather x1, waiting for transfers between devices, on_device(): cols_all = lax.all_gather(by_column, 'gvec', axis=1, tiled=True)[0]  8.62 us
  transfers between devices with their start and end apart: 2, of which 2 were waited for; matrix products, arithmetic and copies ran while one was open for 12% of the time, Pallas kernels for 0%

commit v1 on v0

--- a/solution.py
+++ b/solution.py
@@ -2,6 +2,27 @@
 import jax.numpy as jnp
 from jax import lax
 from jax.sharding import PartitionSpec as P
+
+
+def collect(value, axis, dim):
+    size, index, rows = (lax.axis_size(axis), lax.axis_index(axis), value.shape[dim])
+    right = [(i, (i + 1) % size) for i in range(size)]
+    left = [(i, (i - 1) % size) for i in range(size)]
+    whole = jnp.zeros((*value.shape[:dim], size * rows, *value.shape[dim + 1 :]), value.dtype)
+    whole = lax.dynamic_update_slice_in_dim(whole, value, index * rows, axis=dim)
+    from_left = from_right = value
+    half = size // 2
+    for hop in range(1, half + 1):
+        from_left = lax.ppermute(from_left, axis, right)
+        whole = lax.dynamic_update_slice_in_dim(
+            whole, from_left, (index - hop) % size * rows, axis=dim
+        )
+        if hop < size - half:
+            from_right = lax.ppermute(from_right, axis, left)
+            whole = lax.dynamic_update_slice_in_dim(
+                whole, from_right, (index + hop) % size * rows, axis=dim
+            )
+    return whole
 
 
 def on_device(pairs, cond_energy, val_energy, band_counts, slab):
@@ -21,7 +42,7 @@
     by_block = lax.all_to_all(blocked, "gvec", split_axis=0, concat_axis=2, tiled=True)
     rows_all = lax.all_gather(by_block, "band", axis=3, tiled=True)[0]
     by_column = lax.all_to_all(pairs, "band", split_axis=0, concat_axis=2, tiled=True)
-    cols_all = lax.all_gather(by_column, "gvec", axis=1, tiled=True)[0]
+    cols_all = collect(by_column, "gvec", 1)[0]
     scaled = (weight[:, :, None] * cols_all.astype(jnp.float32)).astype(jnp.bfloat16)
     result = lax.dot_general(
         rows_all, scaled, (((1, 2), (0, 1)), ((), ())), preferred_element_type=jnp.float32

time: 264 us -> 256 us (0.970)
  waiting for transfers between devices: 142 us -> 109 us
  starting transfers between devices: 0.04 us -> 15.3 us
  local copies, waits for them, and re-layouts: 31.7 us -> 41.5 us
    all_gather x1, waiting for transfers between devices: 134 us -> 94 us  [on_device(): rows_all = lax.all_gather(by_block, 'band', axis=3, tiled=True)[0]]
    ppermute x0 -> x7, starting transfers between devices: none -> 15.3 us  [the longest x4 11.5 us: collect(): from_left = lax.ppermute(from_left, axis, right)]
    ppermute x0 -> x7, waiting for transfers between devices: none -> 14.7 us  [the longest x4 14 us: collect(): from_left = lax.ppermute(from_left, axis, right)]
    all_gather x1 -> x0, waiting for transfers between devices: 8.62 us -> none  [on_device(): cols_all = lax.all_gather(by_column, 'gvec', axis=1, tiled=True)[0]]
    dynamic_update_slice x0 -> x8, local copies, waits for them, and re-layouts: none -> 7.24 us  [the longest x4 3.62 us: collect(): lax.dynamic_update_slice_in_dim(whole, from_left, (index - hop) % size *...]
    squeeze x0 -> x1, local copies, waits for them, and re-layouts: none -> 2.76 us  [on_device(): cols_all = collect(by_column, 'gvec', 1)[0]]
  transfers between devices with their start and end apart: 2 -> 8, of which waited for: 2 -> 6; matrix products, arithmetic and copies ran while one was open for 12% -> 5% of each run, Pallas kernels for 0% -> 0%
where the time goes in v1:
time: 256 us; the launch traced here: 255 us
  waiting for transfers between devices  109 us (43%)
  blocking collectives  50.3 us (20%)
  local copies, waits for them, and re-layouts  41.5 us (16%)
  matrix products  23.3 us (9%)
  starting transfers between devices  15.3 us (6%)
  between operations  14.1 us (6%)
    all_gather x1, waiting for transfers between devices, on_device(): rows_all = lax.all_gather(by_block, 'band', axis=3, tiled=True)[0]  94 us
    all_to_all x1, blocking collectives, on_device(): lax.all_to_all(pairs, 'band', split_axis=0, concat_axis=2, tiled=True)  32.5 us
    all_gather x1, local copies, waits for them, and re-layouts, on_device(): rows_all = lax.all_gather(by_block, 'band', axis=3, tiled=True)[0]  30.1 us
    dot_general x1, matrix products, on_device(): lax.dot_general(rows_all, scaled, (((1, 2), (0, 1)), ((), ())), preferred...  23.3 us
    all_to_all x1, blocking collectives, on_device(): lax.all_to_all(blocked, 'gvec', split_axis=0, concat_axis=2, tiled=True)  17.7 us
    ppermute x4, waiting for transfers between devices, collect(): from_left = lax.ppermute(from_left, axis, right)  14 us
    ppermute x4, starting transfers between devices, collect(): from_left = lax.ppermute(from_left, axis, right)  11.5 us
  transfers between devices with their start and end apart: 8, of which 6 were waited for; matrix products, arithmetic and copies ran while one was open for 5% of the time, Pallas kernels for 0%

profile of v1, /device:TPU:1, one launch (start us, length us, event | category | flops | bytes accessed | tf_op | source)
XLA Modules:
  0.0 254.8 jit_solution(16316764549863719596)
XLA Ops:
  6.5 0.0 copy-start
  6.5 0.0 all-gather.3.cloned.1.call-start
  6.5 17.7 %all_to_all.30 = bf16[8,4,1,16,640]{4,3,2,1,0:T(8,128)(2,1)S(1)} all-to-all(bf16[8,4,1,16,640]{4,3,2,1,0:T(8,128)(2,1)} %bitcast.38), channel_id=1, replica_groups=mesh['band'=32,'gvec'=8] {'gvec'}, dimensions={0} | all-to-all | bytes 1310720 | tf_op jit(solution)/shard_map/all_to_all | solution.py:42
  24.3 1.2 copy.8
  25.5 0.0 all-gather.3.cloned.1.call-update
  25.5 32.5 %all_to_all.31 = bf16[32,1,16,640]{3,2,1,0:T(8,128)(2,1)S(1)} all-to-all(bf16[32,1,16,640]{3,2,1,0:T(8,128)(2,1)} %param.5), channel_id=1, replica_groups=mesh['band'=32,'gvec'=8] {'band'}, dimensions={0} | all-to-all | bytes 1310720 | tf_op jit(solution)/shard_map/all_to_all | solution.py:44
  58.1 4.0 %collective-permute-start = (bf16[1,1,512,640]{3,2,1,0:T(8,128)(2,1)S(1)}, bf16[1,1,512,640]{3,2,1,0:T(8,128)(2,1)S(1)}, u32[]{:S(2)}, u32[]{:S(2)}) collective-permute-start(bf16[1,1,512,640]{3,2,1,0:T(8,128)(2,1)S(1)} %bitcast.39), channel_id=1, source_target_pairs={{0,1},{1,2},{2,3},{3,4},{4,5},{5,6},{6,7},{7,0},{8,9},{9,10},{10,1... | collective-permute-start | bytes 1966088 | tf_op jit(solution)/shard_map/ppermute | solution.py:16
  62.1 0.1 collective-permute-start.1
  62.2 7.4 %collective-permute-done = bf16[1,1,512,640]{3,2,1,0:T(8,128)(2,1)S(1)} collective-permute-done((bf16[1,1,512,640]{3,2,1,0:T(8,128)(2,1)S(1)}, bf16[1,1,512,640]{3,2,1,0:T(8,128)(2,1)S(1)}, u32[]{:S(2)}, u32[]{:S(2)}) %collective-permute-start) | collective-permute-done | bytes 655392 | tf_op jit(solution)/shard_map/ppermute | solution.py:16
  69.6 2.5 collective-permute-start.2
  72.7 0.7 iota_compare_fusion
  73.5 0.1 lt.81
  73.6 0.0 copy-done
  73.6 0.2 dynamic-slice_reduce_fusion
  73.8 0.0 collective-permute-done.1
  73.8 1.3 collective-permute-start.3
  75.1 0.8 divide_select_fusion
  75.9 2.8 %squeeze.28 = bf16[8,512,640]{2,1,0:T(8,128)(2,1)} broadcast(bf16[]{:T(256)} %constant.65.clone.1), dimensions={} | broadcast | bytes 5242882 | tf_op jit(solution)/shard_map/squeeze | solution.py:45
  78.7 0.9 constant_dynamic-update-slice_fusion
  79.6 0.0 collective-permute-done.2
  79.6 2.5 collective-permute-start.4
  82.1 0.9 bitcast_dynamic-update-slice_fusion.6
  83.0 0.9 bitcast_dynamic-update-slice_fusion.5
  83.9 0.1 collective-permute-done.3
  84.1 2.4 collective-permute-start.5
  86.5 0.9 bitcast_dynamic-update-slice_fusion.4
  87.4 2.3 collective-permute-done.4
  89.6 2.5 collective-permute-start.6
  92.1 0.9 bitcast_dynamic-update-slice_fusion.3
  93.0 0.9 bitcast_dynamic-update-slice_fusion.2
  94.0 0.5 collective-permute-done.5
  94.5 0.9 bitcast_dynamic-update-slice_fusion.1
  95.4 4.3 %collective-permute-done.6 = bf16[1,1,512,640]{3,2,1,0:T(8,128)(2,1)S(1)} collective-permute-done((bf16[1,1,512,640]{3,2,1,0:T(8,128)(2,1)S(1)}, bf16[1,1,512,640]{3,2,1,0:T(8,128)(2,1)S(1)}, u32[]{:S(2)}, u32[]{:S(2)}) %collective-permute-start.6) | collective-permute-done | bytes 655392 | tf_op jit(solution)/shard_map/ppermute | solution.py:16
  99.7 0.9 bitcast_dynamic-update-slice_fusion
  100.6 94.0 %all-gather.3.cloned.1.call-done = bf16[1,4,8,1,512,640]{5,2,3,1,0,4:T(8,128)(2,1)} async-done(((bf16[1,4,8,1,16,640]{5,2,3,1,0,4:T(8,128)(2,1)}), bf16[1,4,8,1,512,640]{5,2,3,1,0,4:T(8,128)(2,1)}) %all-gather.3.cloned.1.call-update) | async-done | bytes 20971536 | tf_op jit(solution)/shard_map/all_gather | solution.py:43
  194.6 30.1 %copy.9 = bf16[1,4,8,1,512,640]{4,5,2,1,3,0:T(8,128)(2,1)} copy(bf16[1,4,8,1,512,640]{5,2,3,1,0,4:T(8,128)(2,1)} %all-gather.3.cloned.1.call-done) | data formatting | bytes 41943040 | tf_op jit(solution)/shard_map/all_gather | solution.py:43
  224.6 23.3 %fusion = f32[640,4,640,1]{0,2,3,1:T(8,128)} fusion(bf16[1,4,8,1,512,640]{4,5,2,1,3,0:T(8,128)(2,1)} %copy.9, bf16[8,512,640]{2,1,0:T(8,128)(2,1)} %bitcast_dynamic-update-slice_fusion, f32[8,512]{1,0:T(8,128)S(1)} %divide_select_fusion), kind=kOutput, calls=%fused_computation | convolution fusion | flops 13429637120 | bytes 32784384 | tf_op jit(solution)/shard_map/dot_general | solution.py:47
Async XLA Ops:
  6.5 67.0 %copy-start = (f32[32,8]{0,1:T(8,128)S(1)}, f32[32,8]{0,1:T(8,128)}, u32[]{:S(2)}) copy-start(f32[32,8]{0,1:T(8,128)} %param.7) | copy-start | bytes 3076
  6.5 188.0 %all-gather.3.cloned.1.call-start = ((), (), s32[]{:S(2)}) async-start(), calls=%async_computation.2 | async-start | bytes 21626880 | tf_op jit(solution)/shard_map/all_gather | solution.py:43
  58.1 11.6 %collective-permute-start = (bf16[1,1,512,640]{3,2,1,0:T(8,128)(2,1)S(1)}, bf16[1,1,512,640]{3,2,1,0:T(8,128)(2,1)S(1)}, u32[]{:S(2)}, u32[]{:S(2)}) collective-permute-start(bf16[1,1,512,640]{3,2,1,0:T(8,128)(2,1)S(1)} %bitcast.39), channel_id=1, source_target_pairs={{0,1},{1,2},{2,3},{3,4},{4,5},{5,6},{6,7},{7,0},{8,9},{9,10},{10,1... | collective-permute-start | bytes 1966088 | tf_op jit(solution)/shard_map/ppermute | solution.py:16
  62.1 11.7 %collective-permute-start.1 = (bf16[1,1,512,640]{3,2,1,0:T(8,128)(2,1)S(1)}, bf16[1,1,512,640]{3,2,1,0:T(8,128)(2,1)S(1)}, u32[]{:S(2)}, u32[]{:S(2)}) collective-permute-start(bf16[1,1,512,640]{3,2,1,0:T(8,128)(2,1)S(1)} %bitcast.40), channel_id=1, source_target_pairs={{0,7},{1,0},{2,1},{3,2},{4,3},{5,4},{6,5},{7,6},{8,15},{9,8},{10,9... | collective-permute-start | bytes 1966088 | tf_op jit(solution)/shard_map/ppermute | solution.py:21
  69.6 10.0 %collective-permute-start.2 = (bf16[1,1,512,640]{3,2,1,0:T(8,128)(2,1)S(1)}, bf16[1,1,512,640]{3,2,1,0:T(8,128)(2,1)S(1)}, u32[]{:S(2)}, u32[]{:S(2)}) collective-permute-start(bf16[1,1,512,640]{3,2,1,0:T(8,128)(2,1)S(1)} %collective-permute-done), channel_id=1, source_target_pairs={{0,1},{1,2},{2,3},{3,4},{4,5},{5,6},{6,7},{7,0},{8,9},{9,10},{10,1... | collective-permute-start | bytes 1966088 | tf_op jit(solution)/shard_map/ppermute | solution.py:16
  73.8 10.3 %collective-permute-start.3 = (bf16[1,1,512,640]{3,2,1,0:T(8,128)(2,1)S(1)}, bf16[1,1,512,640]{3,2,1,0:T(8,128)(2,1)S(1)}, u32[]{:S(2)}, u32[]{:S(2)}) collective-permute-start(bf16[1,1,512,640]{3,2,1,0:T(8,128)(2,1)S(1)} %collective-permute-done.1), channel_id=1, source_target_pairs={{0,7},{1,0},{2,1},{3,2},{4,3},{5,4},{6,5},{7,6},{8,15},{9,8},{10,9... | collective-permute-start | bytes 1966088 | tf_op jit(solution)/shard_map/ppermute | solution.py:21
  79.6 10.0 %collective-permute-start.4 = (bf16[1,1,512,640]{3,2,1,0:T(8,128)(2,1)S(1)}, bf16[1,1,512,640]{3,2,1,0:T(8,128)(2,1)S(1)}, u32[]{:S(2)}, u32[]{:S(2)}) collective-permute-start(bf16[1,1,512,640]{3,2,1,0:T(8,128)(2,1)S(1)} %collective-permute-done.2), channel_id=1, source_target_pairs={{0,1},{1,2},{2,3},{3,4},{4,5},{5,6},{6,7},{7,0},{8,9},{9,10},{10,1... | collective-permute-start | bytes 1966088 | tf_op jit(solution)/shard_map/ppermute | solution.py:16
  84.1 10.4 %collective-permute-start.5 = (bf16[1,1,512,640]{3,2,1,0:T(8,128)(2,1)S(1)}, bf16[1,1,512,640]{3,2,1,0:T(8,128)(2,1)S(1)}, u32[]{:S(2)}, u32[]{:S(2)}) collective-permute-start(bf16[1,1,512,640]{3,2,1,0:T(8,128)(2,1)S(1)} %collective-permute-done.3), channel_id=1, source_target_pairs={{0,7},{1,0},{2,1},{3,2},{4,3},{5,4},{6,5},{7,6},{8,15},{9,8},{10,9... | collective-permute-start | bytes 1966088 | tf_op jit(solution)/shard_map/ppermute | solution.py:21
  89.6 10.0 %collective-permute-start.6 = (bf16[1,1,512,640]{3,2,1,0:T(8,128)(2,1)S(1)}, bf16[1,1,512,640]{3,2,1,0:T(8,128)(2,1)S(1)}, u32[]{:S(2)}, u32[]{:S(2)}) collective-permute-start(bf16[1,1,512,640]{3,2,1,0:T(8,128)(2,1)S(1)} %collective-permute-done.4), channel_id=1, source_target_pairs={{0,1},{1,2},{2,3},{3,4},{4,5},{5,6},{6,7},{7,0},{8,9},{9,10},{10,1... | collective-permute-start | bytes 1966088 | tf_op jit(solution)/shard_map/ppermute | solution.py:16
Sparse Core Ops, SparseCore 0:
  25.6 168.8 all-gather.2
